TPU v7x, 32 devices: a whole 2x2x4 slice. The times are simulated.
32 devices in a mesh: groups: 2 (over y), ctx: 4 (over z), heads: 2 (over x), rep: 2 (over core).
Axes of the slice: x: 2, y: 2, z: 4, core: 2. Of those that a mesh axis runs over, the one named last changes fastest.
Arguments:
- query_rows: bfloat16 [8192, 1024], P(('groups', 'ctx', 'rep'), 'heads'), parts along dimension 0, may hold values from -6 to 6
- key_rows: bfloat16 [8192, 256], P(('groups', 'ctx', 'rep'), 'heads'), parts along dimension 0, may hold values from -6 to 6
- value_rows: bfloat16 [8192, 256], P(('groups', 'ctx', 'rep'), 'heads'), parts along dimension 0, may hold values from -6 to 6
- attn_out: bfloat16 [8192, 1024], P(('groups', 'ctx', 'rep'), 'heads'), parts along dimension 0, may hold values from -6 to 6
- out_grads: bfloat16 [8192, 1024], P(('groups', 'ctx', 'rep'), 'heads'), parts along dimension 0, may hold values from -36 to 36
- log_sums: float32 [8, 8192], P('heads', ('groups', 'ctx', 'rep')), parts along dimension 1, may hold values from 5.5 to 7.5
- window_offsets: int32 [64, 2], P('groups'), parts along dimension 0, may hold values from 1 to 3, as said below
- summary_ids: int32 [16], P('groups'), parts along dimension 0, may hold values from 0 to 31, as said below
Outputs:
- query_grads: bfloat16 [8192, 1024], P(('groups', 'ctx', 'rep'), 'heads'), parts along dimension 0
- key_grads: bfloat16 [8192, 256], P(('groups', 'ctx', 'rep'), 'heads'), parts along dimension 0
- value_grads: bfloat16 [8192, 256], P(('groups', 'ctx', 'rep'), 'heads'), parts along dimension 0
There are 2 independent parts, one for each index of `groups`. A program takes and returns all parts, laid end to end along the dimension named above; each array names one. Nothing has to cross between parts.
Inputs may be any that keep to these rules, and one draw needn't show every extreme that they name: `window_offsets`: each row holds two different distances, the smaller first; some row holds 1 and 3. `summary_ids`: 8 different block numbers in no particular order; block 0 and block 31 are always among them.
All inputs are finite; a program needn't handle non-finite values.
Results may differ from a plain program's by a relative error of at most 0.0049.
Values may be sent and summed in bfloat16 or wider, within the bound.
No kernel may reach another device: no remote copies, remote signals or barrier semaphores. Data moves between devices by JAX's collectives and lax.ppermute only.
A program may use at most 64 MiB of HBM per device.

v0:
```python
import functools
import math

import jax
import jax.numpy as jnp
from jax import lax
from jax.experimental import pallas as pl
from jax.experimental.pallas import tpu as pltpu
from jax.sharding import PartitionSpec as P

HEAD_DIM = 128
GROUP = 4
BLOCK = 128
REACH = 3
SUMMARY = 8
CORES = 2
SCALE = HEAD_DIM ** (-0.5)
LOG2E = math.log2(math.e)
MICROSECOND = 1_000_000_000
OWN = 10 * MICROSECOND
CAPACITIES = (2, 3, 4, SUMMARY - 1)
F32 = jnp.float32
BF16 = jnp.bfloat16
VMEM = pl.BlockSpec(memory_space=pltpu.VMEM)
SMEM = pl.BlockSpec(memory_space=pltpu.SMEM)
HBM = pl.BlockSpec(memory_space=pltpu.HBM)


def far_rounds(chips):
    rounds = []
    for source in range(chips):
        for target in range(source + 2, chips):
            for senders, receivers, route in rounds:
                if senders.get(source, 0) < CORES and receivers.get(target, 0) < CORES:
                    break
            else:
                senders, receivers, route = {}, {}, []
                rounds.append((senders, receivers, route))
            sent, got = senders.get(source, 0), receivers.get(target, 0)
            route.append((source * CORES + sent, target * CORES + got))
            senders[source], receivers[target] = sent + 1, got + 1
    return [route for _, _, route in rounds]


def table_entry(table, position):
    value = jnp.int32(-1)
    for place, entry in table.items():
        value = jnp.where(position == place, jnp.int32(entry), value)
    return value


def chip_slot(ids_ref, slot, chip_blocks):
    chip = ids_ref[slot] // chip_blocks
    rank = jnp.int32(0)
    for other in range(slot):
        rank += jnp.where(ids_ref[other] // chip_blocks == chip, 1, 0)
    return chip, rank


def chip_count(ids_ref, chip, chip_blocks):
    count = jnp.int32(0)
    for slot in range(SUMMARY):
        count += jnp.where(ids_ref[slot] // chip_blocks == chip, 1, 0)
    return count


def prep_kernel(out_ref, grad_ref, lse_ref, stats_ref):
    stats_ref[...] = jnp.zeros_like(stats_ref)
    for block in range(stats_ref.shape[0]):
        rows = slice(block * BLOCK, (block + 1) * BLOCK)
        for head in range(GROUP):
            columns = slice(head * HEAD_DIM, (head + 1) * HEAD_DIM)
            product = out_ref[rows, columns].astype(F32) * grad_ref[rows, columns].astype(F32)
            stats_ref[block, 0:1, columns] = lse_ref[head : head + 1, rows] * LOG2E
            stats_ref[block, 1:2, columns] = jnp.sum(product.T, axis=0, keepdims=True)


def start_kernel(chips, ids_hbm, key_ref, value_ref, kv_ref, branch_ref, ids_ref, sems):
    chip_blocks = CORES * (key_ref.shape[0] // BLOCK)
    copies = [
        pltpu.make_async_copy(
            ref, kv_ref.at[:, number * HEAD_DIM : (number + 1) * HEAD_DIM], sems.at[number]
        )
        for number, ref in enumerate((key_ref, value_ref))
    ]
    ids_copy = pltpu.make_async_copy(ids_hbm, ids_ref, sems.at[2])
    ids_copy.start()
    for copy in copies:
        copy.start()
    ids_copy.wait()
    most = jnp.int32(0)
    for chip in range(chips - 2):
        most = jnp.maximum(most, chip_count(ids_ref, chip, chip_blocks))
    branch = jnp.int32(0)
    for capacity in capacities(chips)[:-1]:
        branch += jnp.where(most > capacity, 1, 0)
    branch_ref[0] = branch
    for copy in copies:
        copy.wait()


def pick_kernel(ids_ref, own_ref, partner_ref, picked_ref):
    chip = lax.axis_index("ctx")
    core = lax.axis_index("rep")
    blocks_here = own_ref.shape[0] // BLOCK
    chip_blocks = CORES * blocks_here
    capacity = picked_ref.shape[0] // BLOCK
    picked_ref[...] = jnp.zeros_like(picked_ref)
    for slot in range(SUMMARY):
        owner, rank = chip_slot(ids_ref, slot, chip_blocks)
        local = ids_ref[slot] - chip * chip_blocks
        row = pl.multiple_of((local % blocks_here) * BLOCK, BLOCK)
        place = pl.multiple_of(rank * BLOCK, BLOCK)
        mine = local // blocks_here == core
        wanted = (owner == chip) & (rank < capacity)

        @pl.when(wanted & mine)
        def _():
            picked_ref[pl.ds(place, BLOCK), :] = own_ref[pl.ds(row, BLOCK), :]

        @pl.when(wanted & ~mine)
        def _():
            picked_ref[pl.ds(place, BLOCK), :] = partner_ref[pl.ds(row, BLOCK), :]


def nt(a, b):
    return lax.dot_general(a, b, (((1,), (1,)), ((), ())), preferred_element_type=F32)


def nn(a, b):
    return jnp.dot(a, b, preferred_element_type=F32)


def block_grads(keys, values, key_t, query_refs, first, count=1, biases=None, query_at=None):
    query_ref, grad_ref, stats_ref = query_refs
    numbers = [first + step for step in range(count)]
    queries = jnp.concatenate([query_ref[number] for number in numbers], axis=0)
    grads = jnp.concatenate([grad_ref[number] for number in numbers], axis=0)
    log_sums = jnp.concatenate([stats_ref[number, 0:1, :] for number in numbers], axis=1)
    deltas = jnp.concatenate([stats_ref[number, 1:2, :] for number in numbers], axis=1)
    scores = nt(keys, queries) * (SCALE * LOG2E)
    if biases is None:
        probs = jnp.exp2(scores - log_sums)
    else:
        parts = []
        for key, bias in enumerate(biases):
            part = jnp.exp2(scores[key * BLOCK : (key + 1) * BLOCK] - (log_sums + bias))
            if query_at is not None:
                row = lax.broadcasted_iota(jnp.int32, part.shape, 0)
                column = lax.broadcasted_iota(jnp.int32, part.shape, 1) % BLOCK
                part = jnp.where(column - row >= (key - query_at) * BLOCK, part, 0.0)
            parts.append(part)
        probs = jnp.concatenate(parts, axis=0)
    prob_grads = nt(values, grads)
    score_grads = (probs * (prob_grads - deltas) * SCALE).astype(BF16)
    return nn(key_t, score_grads), nn(score_grads, queries), nn(probs.astype(BF16), grads)


def put_queries(to_ref, from_ref, first, dq):
    width = GROUP * BLOCK
    for step in range(dq.shape[1] // width):
        part = dq[:, step * width : (step + 1) * width]
        to_ref[first + step] = from_ref[first + step] + part


def is_summary(ids_ref, key_block):
    found = ids_ref[0] == key_block
    for slot in range(1, SUMMARY):
        found |= ids_ref[slot] == key_block
    return found


def in_window(offsets_ref, query_block, key_block):
    distance = query_block - key_block
    return (distance == offsets_ref[0, query_block]) | (distance == offsets_ref[1, query_block])


def attends(offsets_ref, ids_ref, query_block, key_block):
    chosen = in_window(offsets_ref, query_block, key_block) | is_summary(ids_ref, key_block)
    return (query_block > key_block) & chosen


def keys_of(kv_ref, rows):
    return kv_ref[rows, 0:HEAD_DIM]


def values_of(kv_ref, rows):
    return kv_ref[rows, HEAD_DIM : 2 * HEAD_DIM]


def transposed(keys):
    return keys.astype(F32).T.astype(BF16)


def add_grads(acc_ref, rows, key_part, value_part):
    acc_ref[rows, 0:HEAD_DIM] += key_part
    acc_ref[rows, HEAD_DIM : 2 * HEAD_DIM] += value_part


def places(blocks_here):
    chip = lax.axis_index("ctx")
    base = chip * CORES * blocks_here
    return chip, base, base + lax.axis_index("rep") * blocks_here


def bias_of(flag):
    return jnp.where(flag, 0.0, 1e30).astype(F32)


def near_kernel(
    offsets_ref, ids_ref, kv_ref, q_ref, g_ref, s_ref, local_ref, grads_ref, dq_ref, acc_ref
):
    query_refs = (q_ref, g_ref, s_ref)
    blocks_here = kv_ref.shape[0] // BLOCK
    chip_blocks = CORES * blocks_here
    chip, base, own = places(blocks_here)
    first_key = own - chip_blocks
    acc_ref[...] = jnp.zeros_like(acc_ref)
    dq_ref[0:blocks_here] = jnp.zeros_like(local_ref)
    dq_ref[blocks_here:] = local_ref[...]
    flags = [is_summary(ids_ref, first_key + key) & (chip > 0) for key in range(blocks_here)]
    count = jnp.int32(0)
    chosen = [jnp.int32(0)] * blocks_here
    for key in range(blocks_here):
        for place in range(key + 1):
            chosen[place] = jnp.where(flags[key] & (count == place), key, chosen[place])
        count += jnp.where(flags[key], 1, 0)

    def add(first, count, places_of_keys, biases=None):
        rows = [pl.ds(pl.multiple_of(key * BLOCK, BLOCK), BLOCK) for key in places_of_keys]
        keys = jnp.concatenate([keys_of(kv_ref, row) for row in rows], axis=0)
        values = jnp.concatenate([values_of(kv_ref, row) for row in rows], axis=0)
        dq, dk, dv = block_grads(keys, values, transposed(keys), query_refs, first, count, biases)
        put_queries(dq_ref, dq_ref, first, dq)
        for place, row in enumerate(rows):
            part = slice(place * BLOCK, (place + 1) * BLOCK)
            add_grads(acc_ref, row, dk[part], dv[part])

    def entry(place):
        key = jnp.int32(0)
        for number in range(blocks_here):
            key = jnp.where(place == number, chosen[number], key)
        return key

    odd = lax.rem(count, 2)

    def single_step(item, carry):
        add(item * 4, 4, [chosen[0]])
        return carry

    lax.fori_loop(0, odd * (chip_blocks // 4), single_step, 0)

    def double_step(item, carry):
        turn = odd + 2 * (item // (chip_blocks // 2))
        add(lax.rem(item, chip_blocks // 2) * 2, 2, [entry(turn), entry(turn + 1)])
        return carry

    lax.fori_loop(0, (count // 2) * (chip_blocks // 2), double_step, 0)

    def window_step(number, carry):
        query = base + number
        keys, wanted = [], []
        for place in range(2):
            key = query - offsets_ref[place, query] - first_key
            fits = (key >= 0) & (key < blocks_here)
            key = jnp.where(fits, key, 0)
            for block in range(blocks_here):
                fits &= (key != block) | ~flags[block]
            keys.append(key)
            wanted.append(fits)

        @pl.when(wanted[0] | wanted[1])
        def _():
            add(number + blocks_here, 1, keys, [bias_of(flag) for flag in wanted])

        return carry

    reaches = (chip > 0) & (lax.axis_index("rep") == CORES - 1)
    lax.fori_loop(0, jnp.where(reaches, min(REACH, blocks_here), 0), window_step, 0)
    grads_ref[...] = acc_ref[...].astype(BF16)


def far_kernel(sources, ids_ref, *refs):
    count = len(sources)
    kv_refs, refs = refs[:count], refs[count:]
    query_refs, near_ref, refs = refs[:3], refs[3], refs[4:]
    grads_refs, (dq_ref, partner_ref, acc_ref) = refs[:count], refs[count:]
    chip_blocks = near_ref.shape[0]
    position = lax.axis_index("ctx") * CORES + lax.axis_index("rep")
    capacity = acc_ref.shape[0] // BLOCK
    together = 4 if capacity < 4 else 2 if capacity == 4 else 1
    if count > 1:
        dq_ref[...] = near_ref[...]
        near_ref = dq_ref
    for table, kv_ref, grads_ref in zip(sources, kv_refs, grads_refs):
        held = chip_count(ids_ref, table_entry(table, position), chip_blocks)

        @pl.when(held > 0)
        def _():
            keys, values = keys_of(kv_ref, slice(None)), values_of(kv_ref, slice(None))
            key_t = transposed(keys)
            acc_ref[...] = jnp.zeros_like(acc_ref)

            def query_step(item, carry):
                first = item * together
                dq, dk, dv = block_grads(keys, values, key_t, query_refs, first, together)
                put_queries(dq_ref, near_ref, first, dq)
                add_grads(acc_ref, slice(None), dk, dv)
                return carry

            lax.fori_loop(0, chip_blocks // together, query_step, 0)
            grads_ref[...] = acc_ref[...].astype(BF16)

        @pl.when(held == 0)
        def _():
            grads_ref[...] = jnp.zeros_like(grads_ref)
            if count == 1:
                dq_ref[...] = near_ref[...]

    partner_ref[...] = dq_ref[chip_blocks // CORES :].astype(BF16)


def cross_kernel(
    offsets_ref, ids_ref, kv_ref, q_ref, g_ref, s_ref, pq_ref, pg_ref, ps_ref,
    acc_ref, dq_ref, all_q_ref, all_g_ref, all_s_ref,
):
    blocks_here = kv_ref.shape[0] // BLOCK
    _, base, own = places(blocks_here)
    for from_refs, to_ref in (((q_ref, pq_ref), all_q_ref), ((g_ref, pg_ref), all_g_ref)):
        for side, from_ref in enumerate(from_refs):
            for block in range(blocks_here):
                for head in range(GROUP):
                    to_ref[side * blocks_here + block, head * BLOCK : (head + 1) * BLOCK, :] = from_ref[
                        block * BLOCK : (block + 1) * BLOCK, head * HEAD_DIM : (head + 1) * HEAD_DIM
                    ]
    all_s_ref[0:blocks_here] = s_ref[...]
    all_s_ref[blocks_here:] = ps_ref[...]
    acc_ref[...] = jnp.zeros_like(acc_ref)
    dq_ref[...] = jnp.zeros_like(dq_ref)

    @pl.when(lax.axis_index("rep") == 0)
    def _():
        keys, values = keys_of(kv_ref, slice(None)), values_of(kv_ref, slice(None))
        key_t = transposed(keys)

        def query_step(block, carry):
            number = block + blocks_here
            query = base + number
            flags = [attends(offsets_ref, ids_ref, query, own + key) for key in range(blocks_here)]
            some = flags[0]
            for flag in flags[1:]:
                some |= flag

            @pl.when(some)
            def _():
                dq, dk, dv = block_grads(
                    keys, values, key_t, (all_q_ref, all_g_ref, all_s_ref), number, 1,
                    [bias_of(flag) for flag in flags],
                )
                dq_ref[block] = dq
                add_grads(acc_ref, slice(None), dk, dv)

            return carry

        lax.fori_loop(0, blocks_here, query_step, 0)


def own_kernel(
    offsets_ref, ids_ref, kv_ref, q_ref, g_ref, s_ref, cross_ref, far_ref, acc_ref, dq_ref
):
    blocks_here = kv_ref.shape[0] // BLOCK
    _, _, own = places(blocks_here)
    acc_ref[...] = cross_ref[...]
    keys, values = keys_of(kv_ref, slice(None)), values_of(kv_ref, slice(None))
    key_t = transposed(keys)

    def query_step(block, carry):
        flags = [
            (key >= block) | attends(offsets_ref, ids_ref, own + block, own + key)
            for key in range(blocks_here)
        ]
        dq, dk, dv = block_grads(
            keys, values, key_t, (q_ref, g_ref, s_ref), block, 1,
            [bias_of(flag) for flag in flags], block,
        )
        add_grads(acc_ref, slice(None), dk, dv)
        dq_ref[block] = far_ref[block] + dq
        return carry

    lax.fori_loop(0, blocks_here, query_step, 0)


def query_kernel(own_ref, partner_ref, dq_ref):
    def block_step(block, carry):
        total = own_ref[block] + partner_ref[block].astype(F32)
        rows = pl.ds(pl.multiple_of(block * BLOCK, BLOCK), BLOCK)
        for head in range(GROUP):
            lanes = slice(head * HEAD_DIM, (head + 1) * HEAD_DIM)
            dq_ref[rows, lanes] = total[:, lanes].T.astype(BF16)
        return carry

    lax.fori_loop(0, own_ref.shape[0], block_step, 0)


def final_kernel(last_sender, ids_ref, acc_ref, near_ref, *refs):
    far_refs, (dk_ref, dv_ref, sum_ref) = refs[:-3], refs[-3:]
    blocks_here = acc_ref.shape[0] // BLOCK
    chip_blocks = CORES * blocks_here
    chip = lax.axis_index("ctx")
    core = lax.axis_index("rep")
    sum_ref[...] = acc_ref[...] + near_ref[...].astype(F32)
    dk_ref[...] = keys_of(sum_ref, slice(None)).astype(BF16)
    dv_ref[...] = values_of(sum_ref, slice(None)).astype(BF16)
    capacity = far_refs[0].shape[0] // BLOCK
    for slot in range(SUMMARY):
        owner, rank = chip_slot(ids_ref, slot, chip_blocks)
        local = ids_ref[slot] - chip * chip_blocks - core * blocks_here
        mine = (owner == chip) & (local >= 0) & (local < blocks_here)

        @pl.when(mine & (chip <= last_sender) & (rank < capacity))
        def _():
            rows = pl.ds(pl.multiple_of(local * BLOCK, BLOCK), BLOCK)
            place = pl.ds(pl.multiple_of(rank * BLOCK, BLOCK), BLOCK)
            total = sum_ref[rows, :]
            for far_ref in far_refs:
                total += far_ref[place, :].astype(F32)
            dk_ref[rows, :] = total[:, 0:HEAD_DIM].astype(BF16)
            dv_ref[rows, :] = total[:, HEAD_DIM : 2 * HEAD_DIM].astype(BF16)


def call(kernel, scalars, arrays, out_shape, scratch=(), flops=0, in_space=VMEM, out_specs=None, room=24):
    return pl.pallas_call(
        kernel,
        out_shape=out_shape,
        in_specs=[SMEM] * len(scalars) + [in_space] * len(arrays),
        out_specs=out_specs or jax.tree.map(lambda _: VMEM, out_shape),
        scratch_shapes=list(scratch),
        compiler_params=pltpu.CompilerParams(vmem_limit_bytes=room << 20),
        cost_estimate=pl.CostEstimate(flops=flops, bytes_accessed=0, transcendentals=0),
    )(*scalars, *arrays)


def shape_of(shape, dtype):
    return jax.ShapeDtypeStruct(shape, dtype)


def with_capacity(
    capacity, chips, queries, kv, attn_out, grads, log_sums, window_offsets, summary_ids
):
    rows = queries.shape[0]
    blocks_here = rows // BLOCK
    swap = [(0, 1), (1, 0)]
    up = [(i, i + 1) for i in range(chips - 1)]
    down = [(b, a) for a, b in up]
    routes = far_rounds(chips)
    sources = tuple({b: a // CORES for a, b in route} for route in routes)
    both = ("ctx", "rep")

    kv_partner = lax.ppermute(kv, "rep", swap)
    kv_near = lax.ppermute(kv, "ctx", up)
    far_shape = shape_of((capacity * BLOCK, 2 * HEAD_DIM), BF16)
    picked = call(pick_kernel, (summary_ids,), (kv, kv_partner), far_shape)
    kv_far = [lax.ppermute(picked, both, route) for route in routes]
    attn_out, window_offsets, _ = lax.optimization_barrier((attn_out, window_offsets, picked))
    tables = (window_offsets, summary_ids)
    stats = call(
        prep_kernel, (), (attn_out, grads, log_sums),
        shape_of((blocks_here, 8, GROUP * BLOCK), F32), flops=0,
    )
    own = (queries, grads, stats)
    every = own + tuple(lax.ppermute(x, "rep", swap) for x in own)
    acc_shape = (rows, 2 * HEAD_DIM)
    half_shape = (blocks_here, HEAD_DIM, GROUP * BLOCK)
    chip_blocks = CORES * blocks_here
    dq_shape = shape_of((chip_blocks, *half_shape[1:]), F32)
    stacked_shape = shape_of((chip_blocks, GROUP * BLOCK, HEAD_DIM), BF16)
    cross_acc, cross_dq, *every = call(
        cross_kernel, tables, (kv, *every),
        (
            shape_of(acc_shape, F32), shape_of(half_shape, F32), stacked_shape, stacked_shape,
            shape_of((chip_blocks, *stats.shape[1:]), F32),
        ),
    )
    near_grads, near_dq = call(
        near_kernel, tables, (kv_near, *every, cross_dq), (shape_of(acc_shape, BF16), dq_shape),
        [pltpu.VMEM(acc_shape, F32)],
    )
    *far_grads, far_dq, dq_partner = call(
        functools.partial(far_kernel, sources), (summary_ids,), (*kv_far, *every, near_dq),
        (*[far_shape] * len(routes), dq_shape, shape_of(half_shape, BF16)),
        [pltpu.VMEM(far_shape.shape, F32)], flops=5 * MICROSECOND,
    )
    far_back = [
        lax.ppermute(x, both, [(b, a) for a, b in route]) for x, route in zip(far_grads, routes)
    ]
    near_grads, _ = lax.optimization_barrier((near_grads, far_grads))
    near_back = lax.ppermute(near_grads, "ctx", down)
    dq_partner = lax.ppermute(dq_partner, "rep", swap)
    acc, dq = call(
        own_kernel, tables, (kv, *every, cross_acc, far_dq),
        (shape_of(acc_shape, F32), shape_of(half_shape, F32)), flops=OWN,
    )
    query_grads = call(query_kernel, (), (dq, dq_partner), shape_of(queries.shape, BF16))
    if capacity > 4:
        acc, near_back = lax.optimization_barrier((acc, near_back))
    far_back, acc, query_grads = lax.optimization_barrier((far_back, acc, query_grads))
    far_other = [lax.ppermute(x, "rep", swap) for x in far_back]
    kv_shape = shape_of((rows, HEAD_DIM), BF16)
    key_grads, value_grads = call(
        functools.partial(final_kernel, chips - 3), (summary_ids,),
        (acc, near_back, *far_back, *far_other), (kv_shape, kv_shape),
        [pltpu.VMEM(acc_shape, F32)],
    )
    return query_grads, key_grads, value_grads


def capacities(chips):
    return CAPACITIES if len(far_rounds(chips)) == 1 else CAPACITIES[-1:]


def per_device(chips, queries, keys, values, attn_out, grads, log_sums, window_offsets, summary_ids):
    kv, branch = call(
        functools.partial(start_kernel, chips), (), (summary_ids, keys, values),
        (shape_of((keys.shape[0], 2 * HEAD_DIM), BF16), shape_of((1,), jnp.int32)),
        [pltpu.SMEM(summary_ids.shape, jnp.int32), pltpu.SemaphoreType.DMA((3,))], in_space=HBM, out_specs=(VMEM, SMEM), room=60,
    )
    branches = [functools.partial(with_capacity, limit, chips) for limit in capacities(chips)]
    operands = (queries, kv, attn_out, grads, log_sums, window_offsets.T, summary_ids)
    return lax.switch(branch[0], branches, *operands) if len(branches) > 1 else branches[0](*operands)


def solution(mesh):
    rows = P(("groups", "ctx", "rep"), "heads")
    return jax.shard_map(
        functools.partial(per_device, mesh.shape["ctx"]),
        mesh=mesh,
        in_specs=(rows,) * 5 + (P("heads", ("groups", "ctx", "rep")), P("groups", None), P("groups")),
        out_specs=(rows,) * 3,
        check_vma=False,
    )
```

profile of v0, /device:TPU:12, one launch (start us, length us, event | category | flops | bytes accessed | tf_op | source)
XLA Modules:
  0.0 39.5 jit_solution(16736587455632780220)
XLA Ops:
  0.6 1.5 %shard_map.103 = (bf16[512,256]{1,0:T(8,128)(2,1)S(1)}, s32[1]{0:T(128)}) custom-call(s32[8]{0:T(128)} %ids_hbm.1, bf16[512,128]{1,0:T(8,128)(2,1)} %key_ref.1, bf16[512,128]{1,0:T(8,128)(2,1)} %value_ref.1), custom_call_target="tpu_custom_call" | custom-call | tf_op jit(solution)/shard_map/pallas_call | solution.py:432
  2.8 36.6 %conditional.1 = (bf16[512,512]{1,0:T(8,128)(2,1)}, bf16[512,128]{1,0:T(8,128)(2,1)}, bf16[512,128]{1,0:T(8,128)(2,1)}) conditional(s32[]{:T(128)} %bitcast, (bf16[512,256]{1,0:T(8,128)(2,1)S(1)}, s32[8]{0:T(128)}, bf16[512,512]{1,0:T(8,128)(2,1)}, s32[2,32]{1,0:T(2,128)}, bf16[512,512]{1,0:T(8,128)(2,1)}, ...), branch_computations={%region_0.0_spmd, %region_1.0_spmd, %region_2.0_spmd, %region_3.0_... | conditional | flops 15000000512 | bytes 19400344 | solution.py:529
  2.8 0.0 copy-start.1
  2.8 0.0 copy-start.5
  2.8 0.1 collective-permute-start.12
  2.9 0.5 %collective-permute-start.13 = (bf16[512,512]{1,0:T(8,128)(2,1)}, bf16[512,512]{1,0:T(8,128)(2,1)S(1)}, u32[]{:S(2)}, u32[]{:S(2)}) collective-permute-start(bf16[512,512]{1,0:T(8,128)(2,1)} %get-tuple-element.89.grad_ref.g_ref), channel_id=1, source_target_pairs={{0,1},{1,0},{2,3},{3,2},{4,5},{5,4},{6,7},{7,6},{8,9},{9,8},{10,11... | collective-permute-start | bytes 1572872 | tf_op jit(solution)/shard_map/cond/branch_1_fun/ppermute | solution.py:471
  3.4 0.1 collective-permute-start.10
  3.5 3.5 %collective-permute-start.15 = (bf16[512,256]{1,0:T(8,128)(2,1)S(1)}, bf16[512,256]{1,0:T(8,128)(2,1)S(1)}, u32[]{:S(2)}, u32[]{:S(2)}) collective-permute-start(bf16[512,256]{1,0:T(8,128)(2,1)S(1)} %get-tuple-element.84.own_ref.kv_ref), channel_id=1, source_target_pairs={{0,4},{4,8},{8,12},{1,5},{5,9},{9,13},{2,6},{6,10},{10,14},{3,7},{... | collective-permute-start | bytes 786440 | tf_op jit(solution)/shard_map/cond/branch_1_fun/ppermute | solution.py:460
  7.0 0.0 collective-permute-done.10.partner_ref
  7.0 0.0 copy-start.9
  7.0 0.0 copy-start.13
  7.0 1.2 %branch_1_fun.8 = bf16[384,256]{1,0:T(8,128)(2,1)S(1)} custom-call(s32[8]{0:T(128)} %get-tuple-element.83.ids_ref, bf16[512,256]{1,0:T(8,128)(2,1)S(1)} %get-tuple-element.84.own_ref.kv_ref, bf16[512,256]{1,0:T(8,128)(2,1)S(1)} %collective-permute-done.10.partner_ref), custom_call_target="tpu_custom_call" | custom-call | tf_op jit(solution)/shard_map/cond/branch_1_fun/pallas_call | solution.py:432
  8.2 2.8 %collective-permute-start.11 = (bf16[384,256]{1,0:T(8,128)(2,1)S(1)}, bf16[384,256]{1,0:T(8,128)(2,1)S(1)}, u32[]{:S(2)}, u32[]{:S(2)}) collective-permute-start(bf16[384,256]{1,0:T(8,128)(2,1)S(1)} %branch_1_fun.8), channel_id=1, source_target_pairs={{0,8},{1,12},{4,13},{2,10},{3,14},{6,15},{16,24},{17,28},{20,29},{... | collective-permute-start | bytes 589832 | tf_op jit(solution)/shard_map/cond/branch_1_fun/ppermute | solution.py:463
  11.0 1.5 %branch_1_fun.9.s_ref = f32[4,8,512]{2,1,0:T(8,128)S(1)} custom-call(bf16[512,512]{1,0:T(8,128)(2,1)} %get-tuple-element.90.out_ref, bf16[512,512]{1,0:T(8,128)(2,1)} %get-tuple-element.89.grad_ref.g_ref, f32[4,512]{1,0:T(4,128)} %get-tuple-element.91.lse_ref), custom_call_target="tpu_custom_call" | custom-call | tf_op jit(solution)/shard_map/cond/branch_1_fun/pallas_call | solution.py:432
  12.5 0.1 collective-permute-start.14
  12.6 1.2 %collective-permute-done.14.ps_ref = f32[4,8,512]{2,1,0:T(8,128)S(1)} collective-permute-done((f32[4,8,512]{2,1,0:T(8,128)S(1)}, f32[4,8,512]{2,1,0:T(8,128)S(1)}, u32[]{:S(2)}, u32[]{:S(2)}) %collective-permute-start.14) | collective-permute-done | bytes 65568 | tf_op jit(solution)/shard_map/cond/branch_1_fun/ppermute | solution.py:471
  13.9 0.0 collective-permute-done.12.pq_ref
  13.9 0.0 collective-permute-done.13.pg_ref
  13.9 0.0 copy-done.1
  13.9 0.0 copy-done.5
  13.9 5.0 %branch_1_fun.10 = (f32[512,256]{1,0:T(8,128)S(1)}, f32[4,128,512]{2,1,0:T(8,128)S(1)}, bf16[8,512,128]{2,1,0:T(8,128)(2,1)S(1)}, bf16[8,512,128]{2,1,0:T(8,128)(2,1)S(1)}, f32[8,8,512]{2,1,0:T(8,128)S(1)}) custom-call(s32[2,32]{1,0:T(2,128)} %get-tuple-element.87.offsets_ref, s32[8]{0:T(128)} %get-tuple-element.83.ids_ref, ...), custom_call_target="tpu_custom_call" | custom-call | tf_op jit(solution)/shard_map/cond/branch_1_fun/pallas_call | solution.py:432
  18.9 0.0 collective-permute-done.15.kv_ref
  18.9 0.0 copy-done.9
  18.9 0.0 copy-done.13
  18.9 4.6 %branch_1_fun.11 = (bf16[512,256]{1,0:T(8,128)(2,1)S(1)}, f32[8,128,512]{2,1,0:T(8,128)S(1)}) custom-call(s32[2,32]{1,0:T(2,128)S(1)} %copy-done.13, s32[8]{0:T(128)S(1)} %copy-done.9, bf16[512,256]{1,0:T(8,128)(2,1)S(1)} %collective-permute-done.15.kv_ref, bf16[8,512,128]{2,1,0:T(8,128)(2,1)S(1)} %get-tuple-element.92.q_ref.refs_1_, ...), custom_call_target="tpu_custom_call" | custom-call | tf_op jit(solution)/shard_map/cond/branch_1_fun/pallas_call | solution.py:432
  23.5 0.0 collective-permute-done.11.refs_0_
  23.5 0.8 %branch_1_fun.12 = (bf16[384,256]{1,0:T(8,128)(2,1)S(1)}, f32[8,128,512]{2,1,0:T(8,128)S(1)}, bf16[4,128,512]{2,1,0:T(8,128)(2,1)S(1)}) custom-call(s32[8]{0:T(128)S(1)} %copy-done.9, bf16[384,256]{1,0:T(8,128)(2,1)S(1)} %collective-permute-done.11.refs_0_, bf16[8,512,128]{2,1,0:T(8,128)(2,1)S(1)} %get-tuple-element.92.q_ref.refs_1_, ...), custom_call_target="tpu_custom_call" | custom-call | flops 5000000000 | tf_op jit(solution)/shard_map/cond/branch_1_fun/pallas_call | solution.py:432
  24.3 1.3 %collective-permute-start.16 = (bf16[384,256]{1,0:T(8,128)(2,1)S(1)}, bf16[384,256]{1,0:T(8,128)(2,1)S(1)}, u32[]{:S(2)}, u32[]{:S(2)}) collective-permute-start(bf16[384,256]{1,0:T(8,128)(2,1)S(1)} %get-tuple-element.97), channel_id=1, source_target_pairs={{8,0},{12,1},{13,4},{10,2},{14,3},{15,6},{24,16},{28,17},{29,20},{... | collective-permute-start | bytes 589832 | tf_op jit(solution)/shard_map/cond/branch_1_fun/ppermute | solution.py:494
  25.6 1.9 %collective-permute-start.18 = (bf16[512,256]{1,0:T(8,128)(2,1)S(1)}, bf16[512,256]{1,0:T(8,128)(2,1)S(1)}, u32[]{:S(2)}, u32[]{:S(2)}) collective-permute-start(bf16[512,256]{1,0:T(8,128)(2,1)S(1)} %get-tuple-element.106), channel_id=1, source_target_pairs={{4,0},{8,4},{12,8},{5,1},{9,5},{13,9},{6,2},{10,6},{14,10},{7,3},{... | collective-permute-start | bytes 786440 | tf_op jit(solution)/shard_map/cond/branch_1_fun/ppermute | solution.py:497
  27.6 0.1 collective-permute-start.17
  27.6 4.6 %branch_1_fun.13 = (f32[512,256]{1,0:T(8,128)S(1)}, f32[4,128,512]{2,1,0:T(8,128)S(1)}) custom-call(s32[2,32]{1,0:T(2,128)S(1)} %copy-done.13, s32[8]{0:T(128)S(1)} %copy-done.9, bf16[512,256]{1,0:T(8,128)(2,1)S(1)} %get-tuple-element.84.own_ref.kv_ref, bf16[8,512,128]{2,1,0:T(8,128)(2,1)S(1)} %get-tuple-element.92.q_ref.refs_1_, ...), custom_call_target="tpu_custom_call" | custom-call | flops 10000000000 | tf_op jit(solution)/shard_map/cond/branch_1_fun/pallas_call | solution.py:432
  32.2 0.0 collective-permute-done.17.partner_ref
  32.2 1.2 %branch_1_fun.14 = bf16[512,512]{1,0:T(8,128)(2,1)} custom-call(f32[4,128,512]{2,1,0:T(8,128)S(1)} %get-tuple-element.101.own_ref, bf16[4,128,512]{2,1,0:T(8,128)(2,1)S(1)} %collective-permute-done.17.partner_ref), custom_call_target="tpu_custom_call" | custom-call | tf_op jit(solution)/shard_map/cond/branch_1_fun/pallas_call | solution.py:432
  33.4 0.0 collective-permute-done.16.refs_0_
  33.4 0.5 %collective-permute-start.19 = (bf16[384,256]{1,0:T(8,128)(2,1)S(1)}, bf16[384,256]{1,0:T(8,128)(2,1)S(1)}, u32[]{:S(2)}, u32[]{:S(2)}) collective-permute-start(bf16[384,256]{1,0:T(8,128)(2,1)S(1)} %collective-permute-done.16.refs_0_), channel_id=1, source_target_pairs={{0,1},{1,0},{2,3},{3,2},{4,5},{5,4},{6,7},{7,6},{8,9},{9,8},{10,11... | collective-permute-start | bytes 589832 | tf_op jit(solution)/shard_map/cond/branch_1_fun/ppermute | solution.py:507
  33.9 3.9 %collective-permute-done.18.near_ref = bf16[512,256]{1,0:T(8,128)(2,1)S(1)} collective-permute-done((bf16[512,256]{1,0:T(8,128)(2,1)S(1)}, bf16[512,256]{1,0:T(8,128)(2,1)S(1)}, u32[]{:S(2)}, u32[]{:S(2)}) %collective-permute-start.18) | collective-permute-done | bytes 262176 | tf_op jit(solution)/shard_map/cond/branch_1_fun/ppermute | solution.py:497
  37.8 0.0 collective-permute-done.19.refs_1_
  37.8 1.6 %branch_1_fun.15 = (bf16[512,128]{1,0:T(8,128)(2,1)}, bf16[512,128]{1,0:T(8,128)(2,1)}) custom-call(s32[8]{0:T(128)S(1)} %copy-done.9, f32[512,256]{1,0:T(8,128)S(1)} %get-tuple-element.104.acc_ref, bf16[512,256]{1,0:T(8,128)(2,1)S(1)} %collective-permute-done.18.near_ref, bf16[384,256]{1,0:T(8,128)(2,1)S(1)} %collective-permute-done.16.refs_0_, ...), custom_call_target="tpu_custom_call" | custom-call | tf_op jit(solution)/shard_map/cond/branch_1_fun/pallas_call | solution.py:432
Async XLA Ops:
  2.8 11.0 %copy-start.1 = (bf16[512,512]{1,0:T(8,128)(2,1)S(1)}, bf16[512,512]{1,0:T(8,128)(2,1)}, u32[]{:S(2)}) copy-start(bf16[512,512]{1,0:T(8,128)(2,1)} %get-tuple-element.89.grad_ref.g_ref) | copy-start | bytes 1572868 | tf_op jit(solution)/shard_map/cond
  2.8 11.0 %copy-start.5 = (bf16[512,512]{1,0:T(8,128)(2,1)S(1)}, bf16[512,512]{1,0:T(8,128)(2,1)}, u32[]{:S(2)}) copy-start(bf16[512,512]{1,0:T(8,128)(2,1)} %get-tuple-element.88.q_ref) | copy-start | bytes 1572868 | tf_op jit(solution)/shard_map/cond
  2.8 11.0 %collective-permute-start.12 = (bf16[512,512]{1,0:T(8,128)(2,1)}, bf16[512,512]{1,0:T(8,128)(2,1)S(1)}, u32[]{:S(2)}, u32[]{:S(2)}) collective-permute-start(bf16[512,512]{1,0:T(8,128)(2,1)} %get-tuple-element.88.q_ref), channel_id=1, source_target_pairs={{0,1},{1,0},{2,3},{3,2},{4,5},{5,4},{6,7},{7,6},{8,9},{9,8},{10,11... | collective-permute-start | bytes 1572872 | tf_op jit(solution)/shard_map/cond/branch_1_fun/ppermute | solution.py:471
  2.9 10.9 %collective-permute-start.13 = (bf16[512,512]{1,0:T(8,128)(2,1)}, bf16[512,512]{1,0:T(8,128)(2,1)S(1)}, u32[]{:S(2)}, u32[]{:S(2)}) collective-permute-start(bf16[512,512]{1,0:T(8,128)(2,1)} %get-tuple-element.89.grad_ref.g_ref), channel_id=1, source_target_pairs={{0,1},{1,0},{2,3},{3,2},{4,5},{5,4},{6,7},{7,6},{8,9},{9,8},{10,11... | collective-permute-start | bytes 1572872 | tf_op jit(solution)/shard_map/cond/branch_1_fun/ppermute | solution.py:471
  3.4 3.6 %collective-permute-start.10 = (bf16[512,256]{1,0:T(8,128)(2,1)S(1)}, bf16[512,256]{1,0:T(8,128)(2,1)S(1)}, u32[]{:S(2)}, u32[]{:S(2)}) collective-permute-start(bf16[512,256]{1,0:T(8,128)(2,1)S(1)} %get-tuple-element.84.own_ref.kv_ref), channel_id=1, source_target_pairs={{0,1},{1,0},{2,3},{3,2},{4,5},{5,4},{6,7},{7,6},{8,9},{9,8},{10,11... | collective-permute-start | bytes 786440 | tf_op jit(solution)/shard_map/cond/branch_1_fun/ppermute | solution.py:459
  3.5 15.4 %collective-permute-start.15 = (bf16[512,256]{1,0:T(8,128)(2,1)S(1)}, bf16[512,256]{1,0:T(8,128)(2,1)S(1)}, u32[]{:S(2)}, u32[]{:S(2)}) collective-permute-start(bf16[512,256]{1,0:T(8,128)(2,1)S(1)} %get-tuple-element.84.own_ref.kv_ref), channel_id=1, source_target_pairs={{0,4},{4,8},{8,12},{1,5},{5,9},{9,13},{2,6},{6,10},{10,14},{3,7},{... | collective-permute-start | bytes 786440 | tf_op jit(solution)/shard_map/cond/branch_1_fun/ppermute | solution.py:460
  7.0 11.9 %copy-start.9 = (s32[8]{0:T(128)S(1)}, s32[8]{0:T(128)}, u32[]{:S(2)}) copy-start(s32[8]{0:T(128)} %get-tuple-element.83.ids_ref) | copy-start | bytes 100 | tf_op jit(solution)/shard_map/cond
  7.0 11.9 %copy-start.13 = (s32[2,32]{1,0:T(2,128)S(1)}, s32[2,32]{1,0:T(2,128)}, u32[]{:S(2)}) copy-start(s32[2,32]{1,0:T(2,128)} %get-tuple-element.87.offsets_ref) | copy-start | bytes 772 | tf_op jit(solution)/shard_map/cond
  8.2 15.3 %collective-permute-start.11 = (bf16[384,256]{1,0:T(8,128)(2,1)S(1)}, bf16[384,256]{1,0:T(8,128)(2,1)S(1)}, u32[]{:S(2)}, u32[]{:S(2)}) collective-permute-start(bf16[384,256]{1,0:T(8,128)(2,1)S(1)} %branch_1_fun.8), channel_id=1, source_target_pairs={{0,8},{1,12},{4,13},{2,10},{3,14},{6,15},{16,24},{17,28},{20,29},{... | collective-permute-start | bytes 589832 | tf_op jit(solution)/shard_map/cond/branch_1_fun/ppermute | solution.py:463
  12.5 1.3 %collective-permute-start.14 = (f32[4,8,512]{2,1,0:T(8,128)S(1)}, f32[4,8,512]{2,1,0:T(8,128)S(1)}, u32[]{:S(2)}, u32[]{:S(2)}) collective-permute-start(f32[4,8,512]{2,1,0:T(8,128)S(1)} %branch_1_fun.9.s_ref), channel_id=1, source_target_pairs={{0,1},{1,0},{2,3},{3,2},{4,5},{5,4},{6,7},{7,6},{8,9},{9,8},{10,11... | collective-permute-start | bytes 196616 | tf_op jit(solution)/shard_map/cond/branch_1_fun/ppermute | solution.py:471
  24.3 9.1 %collective-permute-start.16 = (bf16[384,256]{1,0:T(8,128)(2,1)S(1)}, bf16[384,256]{1,0:T(8,128)(2,1)S(1)}, u32[]{:S(2)}, u32[]{:S(2)}) collective-permute-start(bf16[384,256]{1,0:T(8,128)(2,1)S(1)} %get-tuple-element.97), channel_id=1, source_target_pairs={{8,0},{12,1},{13,4},{10,2},{14,3},{15,6},{24,16},{28,17},{29,20},{... | collective-permute-start | bytes 589832 | tf_op jit(solution)/shard_map/cond/branch_1_fun/ppermute | solution.py:494
  25.6 12.2 %collective-permute-start.18 = (bf16[512,256]{1,0:T(8,128)(2,1)S(1)}, bf16[512,256]{1,0:T(8,128)(2,1)S(1)}, u32[]{:S(2)}, u32[]{:S(2)}) collective-permute-start(bf16[512,256]{1,0:T(8,128)(2,1)S(1)} %get-tuple-element.106), channel_id=1, source_target_pairs={{4,0},{8,4},{12,8},{5,1},{9,5},{13,9},{6,2},{10,6},{14,10},{7,3},{... | collective-permute-start | bytes 786440 | tf_op jit(solution)/shard_map/cond/branch_1_fun/ppermute | solution.py:497
  27.6 4.6 %collective-permute-start.17 = (bf16[4,128,512]{2,1,0:T(8,128)(2,1)S(1)}, bf16[4,128,512]{2,1,0:T(8,128)(2,1)S(1)}, u32[]{:S(2)}, u32[]{:S(2)}) collective-permute-start(bf16[4,128,512]{2,1,0:T(8,128)(2,1)S(1)} %get-tuple-element.102), channel_id=1, source_target_pairs={{0,1},{1,0},{2,3},{3,2},{4,5},{5,4},{6,7},{7,6},{8,9},{9,8},{10,11... | collective-permute-start | bytes 1572872 | tf_op jit(solution)/shard_map/cond/branch_1_fun/ppermute | solution.py:498
  33.4 4.4 %collective-permute-start.19 = (bf16[384,256]{1,0:T(8,128)(2,1)S(1)}, bf16[384,256]{1,0:T(8,128)(2,1)S(1)}, u32[]{:S(2)}, u32[]{:S(2)}) collective-permute-start(bf16[384,256]{1,0:T(8,128)(2,1)S(1)} %collective-permute-done.16.refs_0_), channel_id=1, source_target_pairs={{0,1},{1,0},{2,3},{3,2},{4,5},{5,4},{6,7},{7,6},{8,9},{9,8},{10,11... | collective-permute-start | bytes 589832 | tf_op jit(solution)/shard_map/cond/branch_1_fun/ppermute | solution.py:507
where the time goes:
time: 39.9 us; the launch traced here: 39.5 us
  Pallas kernels  22 us (55%)
  starting transfers between devices  10.8 us (27%)
  waiting for transfers between devices  5.12 us (13%)
  between operations  1.34 us (3%)
    pallas_call x9, Pallas kernels, call(): pl.pallas_call(kernel, out_shape=out_shape, in_specs=[SMEM] * len(scalars...  22 us
    ppermute x1, waiting for transfers between devices, with_capacity(): near_back = lax.ppermute(near_grads, 'ctx', down)  3.85 us
    ppermute x1, starting transfers between devices, with_capacity(): kv_near = lax.ppermute(kv, 'ctx', up)  3.47 us
    ppermute x1, starting transfers between devices, with_capacity(): kv_far = [lax.ppermute(picked, both, route) for route in routes]  2.8 us
    ppermute x1, starting transfers between devices, with_capacity(): near_back = lax.ppermute(near_grads, 'ctx', down)  1.92 us
    ppermute x1, starting transfers between devices, with_capacity(): lax.ppermute(x, both, [(b, a) for a, b in route])  1.29 us
    ppermute x3, waiting for transfers between devices, with_capacity(): every = own + tuple((lax.ppermute(x, 'rep', swap) for x in own))  1.25 us
  transfers between devices with their start and end apart: 10, of which 2 were waited for; matrix products, arithmetic and copies ran while one was open for 0% of the time, Pallas kernels for 46%

commit v1 on v0

--- a/solution.py
+++ b/solution.py
@@ -30,16 +30,18 @@
     rounds = []
     for source in range(chips):
         for target in range(source + 2, chips):
-            for senders, receivers, route in rounds:
-                if senders.get(source, 0) < CORES and receivers.get(target, 0) < CORES:
+            wanted = target % CORES
+            for route in rounds:
+                senders = [core for core in range(CORES) if source * CORES + core not in route.values()]
+                receivers = [core for core in range(CORES) if target * CORES + core not in route]
+                if senders and receivers:
                     break
             else:
-                senders, receivers, route = {}, {}, []
-                rounds.append((senders, receivers, route))
-            sent, got = senders.get(source, 0), receivers.get(target, 0)
-            route.append((source * CORES + sent, target * CORES + got))
-            senders[source], receivers[target] = sent + 1, got + 1
-    return [route for _, _, route in rounds]
+                senders, receivers, route = list(range(CORES)), list(range(CORES)), {}
+                rounds.append(route)
+            sender = wanted if wanted in senders else senders[0]
+            route[target * CORES + receivers[0]] = source * CORES + sender
+    return [[(a, b) for b, a in route.items()] for route in rounds]
 
 
 def table_entry(table, position):
@@ -216,8 +218,8 @@
     chip, base, own = places(blocks_here)
     first_key = own - chip_blocks
     acc_ref[...] = jnp.zeros_like(acc_ref)
-    dq_ref[0:blocks_here] = jnp.zeros_like(local_ref)
-    dq_ref[blocks_here:] = local_ref[...]
+    dq_ref[0:blocks_here] = local_ref[...]
+    dq_ref[blocks_here:] = jnp.zeros_like(local_ref)
     flags = [is_summary(ids_ref, first_key + key) & (chip > 0) for key in range(blocks_here)]
     count = jnp.int32(0)
     chosen = [jnp.int32(0)] * blocks_here
@@ -283,7 +285,7 @@
 def far_kernel(sources, ids_ref, *refs):
     count = len(sources)
     kv_refs, refs = refs[:count], refs[count:]
-    query_refs, near_ref, refs = refs[:3], refs[3], refs[4:]
+    query_refs, (near_ref, cross_ref), refs = refs[:3], refs[3:5], refs[5:]
     grads_refs, (dq_ref, partner_ref, acc_ref) = refs[:count], refs[count:]
     chip_blocks = near_ref.shape[0]
     position = lax.axis_index("ctx") * CORES + lax.axis_index("rep")
@@ -317,12 +319,13 @@
             if count == 1:
                 dq_ref[...] = near_ref[...]
 
-    partner_ref[...] = dq_ref[chip_blocks // CORES :].astype(BF16)
+    partner_ref[0 : chip_blocks // CORES] = dq_ref[chip_blocks // CORES :].astype(BF16)
+    partner_ref[chip_blocks // CORES :] = cross_ref[...]
 
 
 def cross_kernel(
     offsets_ref, ids_ref, kv_ref, q_ref, g_ref, s_ref, pq_ref, pg_ref, ps_ref,
-    acc_ref, dq_ref, all_q_ref, all_g_ref, all_s_ref,
+    grads_ref, dq_ref, all_q_ref, all_g_ref, all_s_ref, acc_ref,
 ):
     blocks_here = kv_ref.shape[0] // BLOCK
     _, base, own = places(blocks_here)
@@ -338,15 +341,15 @@
     acc_ref[...] = jnp.zeros_like(acc_ref)
     dq_ref[...] = jnp.zeros_like(dq_ref)
 
-    @pl.when(lax.axis_index("rep") == 0)
+    @pl.when(lax.axis_index("rep") == CORES - 1)
     def _():
         keys, values = keys_of(kv_ref, slice(None)), values_of(kv_ref, slice(None))
         key_t = transposed(keys)
 
         def query_step(block, carry):
-            number = block + blocks_here
-            query = base + number
-            flags = [attends(offsets_ref, ids_ref, query, own + key) for key in range(blocks_here)]
+            flags = [
+                attends(offsets_ref, ids_ref, own + block, base + key) for key in range(blocks_here)
+            ]
             some = flags[0]
             for flag in flags[1:]:
                 some |= flag
@@ -354,7 +357,7 @@
             @pl.when(some)
             def _():
                 dq, dk, dv = block_grads(
-                    keys, values, key_t, (all_q_ref, all_g_ref, all_s_ref), number, 1,
+                    keys, values, key_t, (all_q_ref, all_g_ref, all_s_ref), block, 1,
                     [bias_of(flag) for flag in flags],
                 )
                 dq_ref[block] = dq
@@ -364,13 +367,18 @@
 
         lax.fori_loop(0, blocks_here, query_step, 0)
 
+    for block in range(blocks_here):
+        lanes = slice((block % 2) * 2 * HEAD_DIM, (block % 2 + 1) * 2 * HEAD_DIM)
+        rows = slice(block * BLOCK, (block + 1) * BLOCK)
+        grads_ref[block // 2, :, lanes] = acc_ref[rows, :].astype(BF16)
+
 
 def own_kernel(
-    offsets_ref, ids_ref, kv_ref, q_ref, g_ref, s_ref, cross_ref, far_ref, acc_ref, dq_ref
+    offsets_ref, ids_ref, kv_ref, q_ref, g_ref, s_ref, far_ref, acc_ref, dq_ref
 ):
     blocks_here = kv_ref.shape[0] // BLOCK
     _, _, own = places(blocks_here)
-    acc_ref[...] = cross_ref[...]
+    acc_ref[...] = jnp.zeros_like(acc_ref)
     keys, values = keys_of(kv_ref, slice(None)), values_of(kv_ref, slice(None))
     key_t = transposed(keys)
 
@@ -402,13 +410,17 @@
     lax.fori_loop(0, own_ref.shape[0], block_step, 0)
 
 
-def final_kernel(last_sender, ids_ref, acc_ref, near_ref, *refs):
+def final_kernel(last_sender, ids_ref, acc_ref, near_ref, partner_ref, *refs):
     far_refs, (dk_ref, dv_ref, sum_ref) = refs[:-3], refs[-3:]
     blocks_here = acc_ref.shape[0] // BLOCK
     chip_blocks = CORES * blocks_here
     chip = lax.axis_index("ctx")
     core = lax.axis_index("rep")
-    sum_ref[...] = acc_ref[...] + near_ref[...].astype(F32)
+    for block in range(blocks_here):
+        lanes = slice((block % 2) * 2 * HEAD_DIM, (block % 2 + 1) * 2 * HEAD_DIM)
+        rows = slice(block * BLOCK, (block + 1) * BLOCK)
+        cross = partner_ref[blocks_here + block // 2, :, lanes].astype(F32)
+        sum_ref[rows, :] = acc_ref[rows, :] + near_ref[rows, :].astype(F32) + cross
     dk_ref[...] = keys_of(sum_ref, slice(None)).astype(BF16)
     dv_ref[...] = values_of(sum_ref, slice(None)).astype(BF16)
     capacity = far_refs[0].shape[0] // BLOCK
@@ -472,22 +484,25 @@
     acc_shape = (rows, 2 * HEAD_DIM)
     half_shape = (blocks_here, HEAD_DIM, GROUP * BLOCK)
     chip_blocks = CORES * blocks_here
+    cross_shape = shape_of((blocks_here // 2, BLOCK, 4 * HEAD_DIM), BF16)
+    partner_shape = shape_of((blocks_here + blocks_here // 2, *half_shape[1:]), BF16)
     dq_shape = shape_of((chip_blocks, *half_shape[1:]), F32)
     stacked_shape = shape_of((chip_blocks, GROUP * BLOCK, HEAD_DIM), BF16)
-    cross_acc, cross_dq, *every = call(
-        cross_kernel, tables, (kv, *every),
+    cross_grads, cross_dq, *every = call(
+        cross_kernel, tables, (kv_partner, *every),
         (
-            shape_of(acc_shape, F32), shape_of(half_shape, F32), stacked_shape, stacked_shape,
+            cross_shape, shape_of(half_shape, F32), stacked_shape, stacked_shape,
             shape_of((chip_blocks, *stats.shape[1:]), F32),
         ),
+        [pltpu.VMEM(acc_shape, F32)],
     )
     near_grads, near_dq = call(
         near_kernel, tables, (kv_near, *every, cross_dq), (shape_of(acc_shape, BF16), dq_shape),
         [pltpu.VMEM(acc_shape, F32)],
     )
     *far_grads, far_dq, dq_partner = call(
-        functools.partial(far_kernel, sources), (summary_ids,), (*kv_far, *every, near_dq),
-        (*[far_shape] * len(routes), dq_shape, shape_of(half_shape, BF16)),
+        functools.partial(far_kernel, sources), (summary_ids,), (*kv_far, *every, near_dq, cross_grads),
+        (*[far_shape] * len(routes), dq_shape, partner_shape),
         [pltpu.VMEM(far_shape.shape, F32)], flops=5 * MICROSECOND,
     )
     far_back = [
@@ -497,18 +512,18 @@
     near_back = lax.ppermute(near_grads, "ctx", down)
     dq_partner = lax.ppermute(dq_partner, "rep", swap)
     acc, dq = call(
-        own_kernel, tables, (kv, *every, cross_acc, far_dq),
+        own_kernel, tables, (kv, *every, far_dq),
         (shape_of(acc_shape, F32), shape_of(half_shape, F32)), flops=OWN,
     )
     query_grads = call(query_kernel, (), (dq, dq_partner), shape_of(queries.shape, BF16))
-    if capacity > 4:
+    if capacity > 3:
         acc, near_back = lax.optimization_barrier((acc, near_back))
     far_back, acc, query_grads = lax.optimization_barrier((far_back, acc, query_grads))
     far_other = [lax.ppermute(x, "rep", swap) for x in far_back]
     kv_shape = shape_of((rows, HEAD_DIM), BF16)
     key_grads, value_grads = call(
         functools.partial(final_kernel, chips - 3), (summary_ids,),
-        (acc, near_back, *far_back, *far_other), (kv_shape, kv_shape),
+        (acc, near_back, dq_partner, *far_back, *far_other), (kv_shape, kv_shape),
         [pltpu.VMEM(acc_shape, F32)],
     )
     return query_grads, key_grads, value_grads

time: 39.9 us -> 42.6 us (1.068)
  Pallas kernels: 22 us -> 16.3 us
  waiting for transfers between devices: 5.12 us -> 10.5 us
  starting transfers between devices: 10.8 us -> 13.7 us
    pallas_call x9, Pallas kernels: 22 us -> 16.3 us  [call(): pl.pallas_call(kernel, out_shape=out_shape, in_specs=[SMEM] * len(scalars...]
    ppermute x1, starting transfers between devices: 0.07 us -> 4.02 us  [with_capacity(): dq_partner = lax.ppermute(dq_partner, 'rep', swap)]
    ppermute x1, waiting for transfers between devices: 3.85 us -> 6.8 us  [with_capacity(): near_back = lax.ppermute(near_grads, 'ctx', down)]
    ppermute x1, waiting for transfers between devices: 0.01 us -> 2.83 us  [with_capacity(): kv_near = lax.ppermute(kv, 'ctx', up)]
    ppermute x3, starting transfers between devices: 0.64 us -> 2.88 us  [with_capacity(): every = own + tuple((lax.ppermute(x, 'rep', swap) for x in own))]
    ppermute x1, starting transfers between devices: 2.8 us -> 0.67 us  [with_capacity(): kv_far = [lax.ppermute(picked, both, route) for route in routes]]
    ppermute x1, starting transfers between devices: 1.29 us -> 0.67 us  [with_capacity(): lax.ppermute(x, both, [(b, a) for a, b in route])]
    ppermute x1, starting transfers between devices: 0.49 us -> 0.02 us  [with_capacity(): far_other = [lax.ppermute(x, 'rep', swap) for x in far_back]]
  transfers between devices with their start and end apart: 10 -> 10, of which waited for: 2 -> 3; matrix products, arithmetic and copies ran while one was open for 0% -> 0% of each run, Pallas kernels for 46% -> 29%
where the time goes in v1:
time: 42.6 us; the launch traced here: 42.1 us
  Pallas kernels  16.3 us (38%)
  starting transfers between devices  13.7 us (32%)
  waiting for transfers between devices  10.5 us (25%)
  between operations  1.34 us (3%)
    pallas_call x9, Pallas kernels, call(): pl.pallas_call(kernel, out_shape=out_shape, in_specs=[SMEM] * len(scalars...  16.3 us
    ppermute x1, waiting for transfers between devices, with_capacity(): near_back = lax.ppermute(near_grads, 'ctx', down)  6.8 us
    ppermute x1, starting transfers between devices, with_capacity(): dq_partner = lax.ppermute(dq_partner, 'rep', swap)  4.02 us
    ppermute x1, starting transfers between devices, with_capacity(): kv_near = lax.ppermute(kv, 'ctx', up)  3.47 us
    ppermute x3, starting transfers between devices, with_capacity(): every = own + tuple((lax.ppermute(x, 'rep', swap) for x in own))  2.88 us
    ppermute x1, waiting for transfers between devices, with_capacity(): kv_near = lax.ppermute(kv, 'ctx', up)  2.83 us
    ppermute x1, starting transfers between devices, with_capacity(): near_back = lax.ppermute(near_grads, 'ctx', down)  1.92 us
    ppermute x3, waiting for transfers between devices, with_capacity(): every = own + tuple((lax.ppermute(x, 'rep', swap) for x in own))  0.91 us
  transfers between devices with their start and end apart: 10, of which 3 were waited for; matrix products, arithmetic and copies ran while one was open for 0% of the time, Pallas kernels for 29%

profile of v1, /device:TPU:12, one launch (start us, length us, event | category | flops | bytes accessed | tf_op | source)
XLA Modules:
  0.0 42.1 jit_solution(9393948469221620502)
XLA Ops:
  0.6 1.5 %shard_map.103 = (bf16[512,256]{1,0:T(8,128)(2,1)S(1)}, s32[1]{0:T(128)}) custom-call(s32[8]{0:T(128)} %ids_hbm.1, bf16[512,128]{1,0:T(8,128)(2,1)} %key_ref.1, bf16[512,128]{1,0:T(8,128)(2,1)} %value_ref.1), custom_call_target="tpu_custom_call" | custom-call | tf_op jit(solution)/shard_map/pallas_call | solution.py:444
  2.8 39.3 %conditional.1 = (bf16[512,512]{1,0:T(8,128)(2,1)}, bf16[512,128]{1,0:T(8,128)(2,1)}, bf16[512,128]{1,0:T(8,128)(2,1)}) conditional(s32[]{:T(128)} %bitcast, (bf16[512,256]{1,0:T(8,128)(2,1)S(1)}, s32[8]{0:T(128)}, bf16[512,512]{1,0:T(8,128)(2,1)}, s32[2,32]{1,0:T(2,128)}, bf16[512,512]{1,0:T(8,128)(2,1)}, ...), branch_computations={%region_0.0_spmd, %region_1.0_spmd, %region_2.0_spmd, %region_3.0_... | conditional | flops 15000000512 | bytes 20448920 | solution.py:544
  2.8 0.0 copy-start.1
  2.8 0.0 copy-start.5
  2.8 0.1 collective-permute-start.12
  2.9 0.5 %collective-permute-start.13 = (bf16[512,512]{1,0:T(8,128)(2,1)}, bf16[512,512]{1,0:T(8,128)(2,1)S(1)}, u32[]{:S(2)}, u32[]{:S(2)}) collective-permute-start(bf16[512,512]{1,0:T(8,128)(2,1)} %get-tuple-element.89.grad_ref.g_ref), channel_id=1, source_target_pairs={{0,1},{1,0},{2,3},{3,2},{4,5},{5,4},{6,7},{7,6},{8,9},{9,8},{10,11... | collective-permute-start | bytes 1572872 | tf_op jit(solution)/shard_map/cond/branch_1_fun/ppermute | solution.py:483
  3.4 0.1 collective-permute-start.10
  3.5 3.5 %collective-permute-start.15 = (bf16[512,256]{1,0:T(8,128)(2,1)S(1)}, bf16[512,256]{1,0:T(8,128)(2,1)S(1)}, u32[]{:S(2)}, u32[]{:S(2)}) collective-permute-start(bf16[512,256]{1,0:T(8,128)(2,1)S(1)} %get-tuple-element.84.own_ref.kv_ref), channel_id=1, source_target_pairs={{0,4},{4,8},{8,12},{1,5},{5,9},{9,13},{2,6},{6,10},{10,14},{3,7},{... | collective-permute-start | bytes 786440 | tf_op jit(solution)/shard_map/cond/branch_1_fun/ppermute | solution.py:472
  7.0 0.0 collective-permute-done.10.partner_ref.kv_ref
  7.0 0.0 copy-start.9
  7.0 0.0 copy-start.13
  7.0 1.2 %branch_1_fun.8 = bf16[384,256]{1,0:T(8,128)(2,1)S(1)} custom-call(s32[8]{0:T(128)} %get-tuple-element.83.ids_ref, bf16[512,256]{1,0:T(8,128)(2,1)S(1)} %get-tuple-element.84.own_ref.kv_ref, bf16[512,256]{1,0:T(8,128)(2,1)S(1)} %collective-permute-done.10.partner_ref.kv_ref), custom_call_target="tpu_custom_call" | custom-call | tf_op jit(solution)/shard_map/cond/branch_1_fun/pallas_call | solution.py:444
  8.2 0.7 %collective-permute-start.11 = (bf16[384,256]{1,0:T(8,128)(2,1)S(1)}, bf16[384,256]{1,0:T(8,128)(2,1)S(1)}, u32[]{:S(2)}, u32[]{:S(2)}) collective-permute-start(bf16[384,256]{1,0:T(8,128)(2,1)S(1)} %branch_1_fun.8), channel_id=1, source_target_pairs={{0,8},{1,12},{5,13},{2,10},{3,14},{7,15},{16,24},{17,28},{21,29},{... | collective-permute-start | bytes 589832 | tf_op jit(solution)/shard_map/cond/branch_1_fun/ppermute | solution.py:475
  8.9 1.5 %branch_1_fun.9.s_ref = f32[4,8,512]{2,1,0:T(8,128)S(1)} custom-call(bf16[512,512]{1,0:T(8,128)(2,1)} %get-tuple-element.90.out_ref, bf16[512,512]{1,0:T(8,128)(2,1)} %get-tuple-element.89.grad_ref.g_ref, f32[4,512]{1,0:T(4,128)} %get-tuple-element.91.lse_ref), custom_call_target="tpu_custom_call" | custom-call | tf_op jit(solution)/shard_map/cond/branch_1_fun/pallas_call | solution.py:444
  10.4 2.3 %collective-permute-start.14 = (f32[4,8,512]{2,1,0:T(8,128)S(1)}, f32[4,8,512]{2,1,0:T(8,128)S(1)}, u32[]{:S(2)}, u32[]{:S(2)}) collective-permute-start(f32[4,8,512]{2,1,0:T(8,128)S(1)} %branch_1_fun.9.s_ref), channel_id=1, source_target_pairs={{0,1},{1,0},{2,3},{3,2},{4,5},{5,4},{6,7},{7,6},{8,9},{9,8},{10,11... | collective-permute-start | bytes 196616 | tf_op jit(solution)/shard_map/cond/branch_1_fun/ppermute | solution.py:483
  12.7 0.9 %collective-permute-done.14.ps_ref = f32[4,8,512]{2,1,0:T(8,128)S(1)} collective-permute-done((f32[4,8,512]{2,1,0:T(8,128)S(1)}, f32[4,8,512]{2,1,0:T(8,128)S(1)}, u32[]{:S(2)}, u32[]{:S(2)}) %collective-permute-start.14) | collective-permute-done | bytes 65568 | tf_op jit(solution)/shard_map/cond/branch_1_fun/ppermute | solution.py:483
  13.6 0.0 collective-permute-done.12.pq_ref
  13.6 0.0 collective-permute-done.13.pg_ref
  13.6 0.0 copy-done.1
  13.6 0.0 copy-done.5
  13.6 1.2 %branch_1_fun.10 = (bf16[2,128,512]{2,1,0:T(8,128)(2,1)S(1)}, f32[4,128,512]{2,1,0:T(8,128)S(1)}, bf16[8,512,128]{2,1,0:T(8,128)(2,1)S(1)}, bf16[8,512,128]{2,1,0:T(8,128)(2,1)S(1)}, f32[8,8,512]{2,1,0:T(8,128)S(1)}) custom-call(s32[2,32]{1,0:T(2,128)} %get-tuple-element.87.offsets_ref, s32[8]{0:T(128)} %get-tuple-element.83.ids_ref, ...), custom_call_target="tpu_custom_call" | custom-call | tf_op jit(solution)/shard_map/cond/branch_1_fun/pallas_call | solution.py:444
  14.8 2.8 %collective-permute-done.15.kv_ref = bf16[512,256]{1,0:T(8,128)(2,1)S(1)} collective-permute-done((bf16[512,256]{1,0:T(8,128)(2,1)S(1)}, bf16[512,256]{1,0:T(8,128)(2,1)S(1)}, u32[]{:S(2)}, u32[]{:S(2)}) %collective-permute-start.15) | collective-permute-done | bytes 262176 | tf_op jit(solution)/shard_map/cond/branch_1_fun/ppermute | solution.py:472
  17.7 0.0 copy-done.9
  17.7 0.0 copy-done.13
  17.7 2.7 %branch_1_fun.11 = (bf16[512,256]{1,0:T(8,128)(2,1)S(1)}, f32[8,128,512]{2,1,0:T(8,128)S(1)}) custom-call(s32[2,32]{1,0:T(2,128)S(1)} %copy-done.13, s32[8]{0:T(128)S(1)} %copy-done.9, bf16[512,256]{1,0:T(8,128)(2,1)S(1)} %collective-permute-done.15.kv_ref, bf16[8,512,128]{2,1,0:T(8,128)(2,1)S(1)} %get-tuple-element.92.q_ref.refs_1_, ...), custom_call_target="tpu_custom_call" | custom-call | tf_op jit(solution)/shard_map/cond/branch_1_fun/pallas_call | solution.py:444
  20.4 0.0 collective-permute-done.11.refs_0_
  20.4 0.8 %branch_1_fun.12 = (bf16[384,256]{1,0:T(8,128)(2,1)S(1)}, f32[8,128,512]{2,1,0:T(8,128)S(1)}, bf16[6,128,512]{2,1,0:T(8,128)(2,1)S(1)}) custom-call(s32[8]{0:T(128)S(1)} %copy-done.9, bf16[384,256]{1,0:T(8,128)(2,1)S(1)} %collective-permute-done.11.refs_0_, bf16[8,512,128]{2,1,0:T(8,128)(2,1)S(1)} %get-tuple-element.92.q_ref.refs_1_, ...), custom_call_target="tpu_custom_call" | custom-call | flops 5000000000 | tf_op jit(solution)/shard_map/cond/branch_1_fun/pallas_call | solution.py:444
  21.2 0.7 %collective-permute-start.16 = (bf16[384,256]{1,0:T(8,128)(2,1)S(1)}, bf16[384,256]{1,0:T(8,128)(2,1)S(1)}, u32[]{:S(2)}, u32[]{:S(2)}) collective-permute-start(bf16[384,256]{1,0:T(8,128)(2,1)S(1)} %get-tuple-element.98), channel_id=1, source_target_pairs={{8,0},{12,1},{13,5},{10,2},{14,3},{15,7},{24,16},{28,17},{29,21},{... | collective-permute-start | bytes 589832 | tf_op jit(solution)/shard_map/cond/branch_1_fun/ppermute | solution.py:509
  21.9 1.9 %collective-permute-start.18 = (bf16[512,256]{1,0:T(8,128)(2,1)S(1)}, bf16[512,256]{1,0:T(8,128)(2,1)S(1)}, u32[]{:S(2)}, u32[]{:S(2)}) collective-permute-start(bf16[512,256]{1,0:T(8,128)(2,1)S(1)} %get-tuple-element.106), channel_id=1, source_target_pairs={{4,0},{8,4},{12,8},{5,1},{9,5},{13,9},{6,2},{10,6},{14,10},{7,3},{... | collective-permute-start | bytes 786440 | tf_op jit(solution)/shard_map/cond/branch_1_fun/ppermute | solution.py:512
  23.8 4.0 %collective-permute-start.17 = (bf16[6,128,512]{2,1,0:T(8,128)(2,1)S(1)}, bf16[6,128,512]{2,1,0:T(8,128)(2,1)S(1)}, u32[]{:S(2)}, u32[]{:S(2)}) collective-permute-start(bf16[6,128,512]{2,1,0:T(8,128)(2,1)S(1)} %get-tuple-element.102), channel_id=1, source_target_pairs={{0,1},{1,0},{2,3},{3,2},{4,5},{5,4},{6,7},{7,6},{8,9},{9,8},{10,11... | collective-permute-start | bytes 2359304 | tf_op jit(solution)/shard_map/cond/branch_1_fun/ppermute | solution.py:513
  27.8 4.5 %branch_1_fun.13 = (f32[512,256]{1,0:T(8,128)S(1)}, f32[4,128,512]{2,1,0:T(8,128)S(1)}) custom-call(s32[2,32]{1,0:T(2,128)S(1)} %copy-done.13, s32[8]{0:T(128)S(1)} %copy-done.9, bf16[512,256]{1,0:T(8,128)(2,1)S(1)} %get-tuple-element.84.own_ref.kv_ref, bf16[8,512,128]{2,1,0:T(8,128)(2,1)S(1)} %get-tuple-element.92.q_ref.refs_1_, ...), custom_call_target="tpu_custom_call" | custom-call | flops 10000000000 | tf_op jit(solution)/shard_map/cond/branch_1_fun/pallas_call | solution.py:444
  32.4 0.0 collective-permute-done.17.partner_ref
  32.4 1.2 %branch_1_fun.14 = bf16[512,512]{1,0:T(8,128)(2,1)} custom-call(f32[4,128,512]{2,1,0:T(8,128)S(1)} %get-tuple-element.101.own_ref, bf16[6,128,512]{2,1,0:T(8,128)(2,1)S(1)} %collective-permute-done.17.partner_ref), custom_call_target="tpu_custom_call" | custom-call | tf_op jit(solution)/shard_map/cond/branch_1_fun/pallas_call | solution.py:444
  33.6 0.0 collective-permute-done.16.refs_0_
  33.6 0.0 collective-permute-start.19
  33.7 6.8 %collective-permute-done.18.near_ref = bf16[512,256]{1,0:T(8,128)(2,1)S(1)} collective-permute-done((bf16[512,256]{1,0:T(8,128)(2,1)S(1)}, bf16[512,256]{1,0:T(8,128)(2,1)S(1)}, u32[]{:S(2)}, u32[]{:S(2)}) %collective-permute-start.18) | collective-permute-done | bytes 262176 | tf_op jit(solution)/shard_map/cond/branch_1_fun/ppermute | solution.py:512
  40.5 0.0 collective-permute-done.19.refs_1_
  40.5 1.6 %branch_1_fun.15 = (bf16[512,128]{1,0:T(8,128)(2,1)}, bf16[512,128]{1,0:T(8,128)(2,1)}) custom-call(s32[8]{0:T(128)S(1)} %copy-done.9, f32[512,256]{1,0:T(8,128)S(1)} %get-tuple-element.104.acc_ref, bf16[512,256]{1,0:T(8,128)(2,1)S(1)} %collective-permute-done.18.near_ref, bf16[6,128,512]{2,1,0:T(8,128)(2,1)S(1)} %collective-permute-done.17.partner_ref, ...), custom_call_target="tpu_custom_call" | custom-call | tf_op jit(solution)/shard_map/cond/branch_1_fun/pallas_call | solution.py:444
Async XLA Ops:
  2.8 10.8 %copy-start.1 = (bf16[512,512]{1,0:T(8,128)(2,1)S(1)}, bf16[512,512]{1,0:T(8,128)(2,1)}, u32[]{:S(2)}) copy-start(bf16[512,512]{1,0:T(8,128)(2,1)} %get-tuple-element.89.grad_ref.g_ref) | copy-start | bytes 1572868 | tf_op jit(solution)/shard_map/cond
  2.8 10.8 %copy-start.5 = (bf16[512,512]{1,0:T(8,128)(2,1)S(1)}, bf16[512,512]{1,0:T(8,128)(2,1)}, u32[]{:S(2)}) copy-start(bf16[512,512]{1,0:T(8,128)(2,1)} %get-tuple-element.88.q_ref) | copy-start | bytes 1572868 | tf_op jit(solution)/shard_map/cond
  2.8 10.8 %collective-permute-start.12 = (bf16[512,512]{1,0:T(8,128)(2,1)}, bf16[512,512]{1,0:T(8,128)(2,1)S(1)}, u32[]{:S(2)}, u32[]{:S(2)}) collective-permute-start(bf16[512,512]{1,0:T(8,128)(2,1)} %get-tuple-element.88.q_ref), channel_id=1, source_target_pairs={{0,1},{1,0},{2,3},{3,2},{4,5},{5,4},{6,7},{7,6},{8,9},{9,8},{10,11... | collective-permute-start | bytes 1572872 | tf_op jit(solution)/shard_map/cond/branch_1_fun/ppermute | solution.py:483
  2.9 10.7 %collective-permute-start.13 = (bf16[512,512]{1,0:T(8,128)(2,1)}, bf16[512,512]{1,0:T(8,128)(2,1)S(1)}, u32[]{:S(2)}, u32[]{:S(2)}) collective-permute-start(bf16[512,512]{1,0:T(8,128)(2,1)} %get-tuple-element.89.grad_ref.g_ref), channel_id=1, source_target_pairs={{0,1},{1,0},{2,3},{3,2},{4,5},{5,4},{6,7},{7,6},{8,9},{9,8},{10,11... | collective-permute-start | bytes 1572872 | tf_op jit(solution)/shard_map/cond/branch_1_fun/ppermute | solution.py:483
  3.4 3.6 %collective-permute-start.10 = (bf16[512,256]{1,0:T(8,128)(2,1)S(1)}, bf16[512,256]{1,0:T(8,128)(2,1)S(1)}, u32[]{:S(2)}, u32[]{:S(2)}) collective-permute-start(bf16[512,256]{1,0:T(8,128)(2,1)S(1)} %get-tuple-element.84.own_ref.kv_ref), channel_id=1, source_target_pairs={{0,1},{1,0},{2,3},{3,2},{4,5},{5,4},{6,7},{7,6},{8,9},{9,8},{10,11... | collective-permute-start | bytes 786440 | tf_op jit(solution)/shard_map/cond/branch_1_fun/ppermute | solution.py:471
  3.5 14.2 %collective-permute-start.15 = (bf16[512,256]{1,0:T(8,128)(2,1)S(1)}, bf16[512,256]{1,0:T(8,128)(2,1)S(1)}, u32[]{:S(2)}, u32[]{:S(2)}) collective-permute-start(bf16[512,256]{1,0:T(8,128)(2,1)S(1)} %get-tuple-element.84.own_ref.kv_ref), channel_id=1, source_target_pairs={{0,4},{4,8},{8,12},{1,5},{5,9},{9,13},{2,6},{6,10},{10,14},{3,7},{... | collective-permute-start | bytes 786440 | tf_op jit(solution)/shard_map/cond/branch_1_fun/ppermute | solution.py:472
  7.0 10.7 %copy-start.9 = (s32[8]{0:T(128)S(1)}, s32[8]{0:T(128)}, u32[]{:S(2)}) copy-start(s32[8]{0:T(128)} %get-tuple-element.83.ids_ref) | copy-start | bytes 100 | tf_op jit(solution)/shard_map/cond
  7.0 10.7 %copy-start.13 = (s32[2,32]{1,0:T(2,128)S(1)}, s32[2,32]{1,0:T(2,128)}, u32[]{:S(2)}) copy-start(s32[2,32]{1,0:T(2,128)} %get-tuple-element.87.offsets_ref) | copy-start | bytes 772 | tf_op jit(solution)/shard_map/cond
  8.2 12.2 %collective-permute-start.11 = (bf16[384,256]{1,0:T(8,128)(2,1)S(1)}, bf16[384,256]{1,0:T(8,128)(2,1)S(1)}, u32[]{:S(2)}, u32[]{:S(2)}) collective-permute-start(bf16[384,256]{1,0:T(8,128)(2,1)S(1)} %branch_1_fun.8), channel_id=1, source_target_pairs={{0,8},{1,12},{5,13},{2,10},{3,14},{7,15},{16,24},{17,28},{21,29},{... | collective-permute-start | bytes 589832 | tf_op jit(solution)/shard_map/cond/branch_1_fun/ppermute | solution.py:475
  10.4 3.2 %collective-permute-start.14 = (f32[4,8,512]{2,1,0:T(8,128)S(1)}, f32[4,8,512]{2,1,0:T(8,128)S(1)}, u32[]{:S(2)}, u32[]{:S(2)}) collective-permute-start(f32[4,8,512]{2,1,0:T(8,128)S(1)} %branch_1_fun.9.s_ref), channel_id=1, source_target_pairs={{0,1},{1,0},{2,3},{3,2},{4,5},{5,4},{6,7},{7,6},{8,9},{9,8},{10,11... | collective-permute-start | bytes 196616 | tf_op jit(solution)/shard_map/cond/branch_1_fun/ppermute | solution.py:483
  21.2 12.4 %collective-permute-start.16 = (bf16[384,256]{1,0:T(8,128)(2,1)S(1)}, bf16[384,256]{1,0:T(8,128)(2,1)S(1)}, u32[]{:S(2)}, u32[]{:S(2)}) collective-permute-start(bf16[384,256]{1,0:T(8,128)(2,1)S(1)} %get-tuple-element.98), channel_id=1, source_target_pairs={{8,0},{12,1},{13,5},{10,2},{14,3},{15,7},{24,16},{28,17},{29,21},{... | collective-permute-start | bytes 589832 | tf_op jit(solution)/shard_map/cond/branch_1_fun/ppermute | solution.py:509
  21.9 18.6 %collective-permute-start.18 = (bf16[512,256]{1,0:T(8,128)(2,1)S(1)}, bf16[512,256]{1,0:T(8,128)(2,1)S(1)}, u32[]{:S(2)}, u32[]{:S(2)}) collective-permute-start(bf16[512,256]{1,0:T(8,128)(2,1)S(1)} %get-tuple-element.106), channel_id=1, source_target_pairs={{4,0},{8,4},{12,8},{5,1},{9,5},{13,9},{6,2},{10,6},{14,10},{7,3},{... | collective-permute-start | bytes 786440 | tf_op jit(solution)/shard_map/cond/branch_1_fun/ppermute | solution.py:512
  23.8 8.6 %collective-permute-start.17 = (bf16[6,128,512]{2,1,0:T(8,128)(2,1)S(1)}, bf16[6,128,512]{2,1,0:T(8,128)(2,1)S(1)}, u32[]{:S(2)}, u32[]{:S(2)}) collective-permute-start(bf16[6,128,512]{2,1,0:T(8,128)(2,1)S(1)} %get-tuple-element.102), channel_id=1, source_target_pairs={{0,1},{1,0},{2,3},{3,2},{4,5},{5,4},{6,7},{7,6},{8,9},{9,8},{10,11... | collective-permute-start | bytes 2359304 | tf_op jit(solution)/shard_map/cond/branch_1_fun/ppermute | solution.py:513
  33.6 6.8 %collective-permute-start.19 = (bf16[384,256]{1,0:T(8,128)(2,1)S(1)}, bf16[384,256]{1,0:T(8,128)(2,1)S(1)}, u32[]{:S(2)}, u32[]{:S(2)}) collective-permute-start(bf16[384,256]{1,0:T(8,128)(2,1)S(1)} %collective-permute-done.16.refs_0_), channel_id=1, source_target_pairs={{0,1},{1,0},{2,3},{3,2},{4,5},{5,4},{6,7},{7,6},{8,9},{9,8},{10,11... | collective-permute-start | bytes 589832 | tf_op jit(solution)/shard_map/cond/branch_1_fun/ppermute | solution.py:522
